TPU v7x, 512 devices: a whole 4x4x16 slice. The times are simulated.
512 devices in a mesh: row: 16 (over z), col: 32 (over x, y, core).
Axes of the slice: x: 4, y: 4, z: 16, core: 2. Of those that a mesh axis runs over, the one named last changes fastest.
Arguments:
- coords: float32 [3, 65536], P(None, ('row', 'col')), may hold values from -1 to 1
- residual_in: float32 [65536, 512], P(('row', 'col')), may hold values from -6 to 6
- link_mask: int32 [512, 2], P(('row', 'col')), may hold values 0 or 1
- compress: float32 [65536, 256], P(('row', 'col')), may hold values from -0.5 to 0.5
- expand: float32 [65536, 256], P(('row', 'col')), may hold values from -0.375 to 0.375
- level_gain: float32 [512, 1280], P(('row', 'col')), may hold values from 0.5 to 1.5
- level_couple: float32 [131072, 1280], P(('row', 'col')), may hold values from -0.1875 to 0.1875
- partner_perm: int32 [512, 5, 256], P(('row', 'col')), may hold values from 0 to 255, each once within a row
Outputs:
- new_residual: float32 [65536, 512], P(('row', 'col'))
- res_norms: float32 [512], replicated
Inputs may be any that keep to these rules, and one draw needn't show every extreme that they name: `partner_perm`: each row of 256 entries names every number once.
All inputs are finite; a program needn't handle non-finite values. No bound on the sum of `link_mask` on one device may be relied on, other than what follows from the above.
Results may differ from a plain program's by a relative error of at most 0.0003.
Values sent between devices are 32-bit elements; how exact they have to be, the bound alone decides.
No kernel may reach another device: no remote copies, remote signals or barrier semaphores. Data moves between devices by JAX's collectives and lax.ppermute only.
A program may use at most 64 MiB of HBM per device.

v0:
```python
import jax
import jax.numpy as jnp
from jax import lax
from jax.sharding import PartitionSpec as P

ROW_LEVELS = 2
COL_LEVELS = 3
WAVENUM = 6.0
SOFTEN = 0.01


def in_blocks(shard, dim, length):
    shape = shard.shape
    tiles = shard.reshape(*shape[:dim], length, shape[dim] // length, *shape[dim + 1 :])
    return jnp.moveaxis(tiles, dim, 0)


def sent_and_summed(shard, axis, dim):
    length = lax.axis_size(axis)
    tiles = lax.all_to_all(in_blocks(shard, dim, length), axis, 0, 0, tiled=True)
    return jnp.sum(tiles, axis=0)


def side_by_side(arrays, axis, dim, along):
    widths = [a.shape[along] for a in arrays]
    both = jnp.concatenate(arrays, axis=along)
    whole = sent_and_summed(both, axis, dim)
    return tuple(jnp.split(whole, [sum(widths[:k]) for k in range(1, len(widths))], axis=along))


def from_everyone(shard, axis):
    length = lax.axis_size(axis)
    return lax.all_to_all(
        jnp.broadcast_to(shard[None], (length, *shard.shape)), axis, 0, 0, tiled=True
    )


def over_copies(shard, axis):
    return from_everyone(shard, axis).sum(axis=0)


def packed_total(arrays, axis):
    ends = [0]
    for a in arrays:
        ends.append(ends[-1] + a.size)
    so_far = over_copies(jnp.concatenate([a.ravel() for a in arrays]), axis)
    return tuple((so_far[b:e].reshape(a.shape) for a, b, e in zip(arrays, ends, ends[1:])))


def gather_turned(arrays, axis, dims):
    turned = [jnp.moveaxis(a, dim, 0) for a, dim in zip(arrays, dims)]
    both = jnp.concatenate([t.reshape(len(t), -1) for t in turned], axis=1)
    whole, at, finished = (lax.all_gather(both, axis, axis=0, tiled=True), 0, [])
    for t, dim in zip(turned, dims):
        piece = whole[:, at : at + t[0].size].reshape(-1, *t.shape[1:])
        finished.append(jnp.moveaxis(piece, 0, dim))
        at += t[0].size
    return tuple(finished)


def from_behind(block, axis, distance):
    devices = range(lax.axis_size(axis))
    route = [(i - distance, i) for i in devices if i - distance in devices]
    return lax.ppermute(block, axis, route)


def from_partner(block, axis, distance):
    count = lax.axis_size(axis)
    route = []
    for low in range(count):
        high = low | 1 << distance
        if high != low and high < count:
            route += [(low, high), (high, low)]
    return lax.ppermute(block, axis, route)


def kernel_tile(own_xyz, other_xyz):
    dist_sq = (own_xyz[0][:, None] - other_xyz[0][None, :]) ** 2
    dist_sq = dist_sq + (own_xyz[1][:, None] - other_xyz[1][None, :]) ** 2
    dist_sq = dist_sq + (own_xyz[2][:, None] - other_xyz[2][None, :]) ** 2
    return jnp.cos(WAVENUM * jnp.sqrt(dist_sq)) / jnp.sqrt(dist_sq + SOFTEN)


def matmul_hi(left, right):
    return jnp.dot(left, right, precision=lax.Precision.HIGHEST)


def inner_cols(left, right):
    return lax.dot_general(left, right, (((0,), (0,)), ((), ())), precision=lax.Precision.HIGHEST)


def chol_solve(gram_mat, cross_mat):
    factor = jnp.linalg.cholesky(gram_mat)
    middle = lax.linalg.triangular_solve(factor, cross_mat, left_side=True, lower=True)
    return lax.linalg.triangular_solve(factor, middle, left_side=True, lower=True, transpose_a=True)


def global_sum(members):
    shares = side_by_side((members[0], members[1], members[2]), "col", 1, 0)
    shares = packed_total((shares[0], shares[1], shares[2]), "row")
    return gather_turned((shares[0], shares[1], shares[2]), "col", (1, 1, 1))


def shards(
    coords, residual_in, link_mask, compress, expand, level_gain, level_couple, partner_perm
):
    below_xyz, below_rhs = from_behind((coords, residual_in), ("row", "col"), 1)
    above_xyz, above_rhs = from_behind((coords, residual_in), ("row", "col"), -1)
    rank_width = compress.shape[1]
    coeffs = inner_cols(compress, residual_in)

    def mix_level(current, partner, level_at):
        taken_rows = partner_perm[0, level_at]
        picked = jnp.take(partner, taken_rows, axis=0)
        gain_col = level_gain[0, level_at * rank_width : (level_at + 1) * rank_width][:, None]
        couple = level_couple[:, level_at * rank_width : (level_at + 1) * rank_width]
        return gain_col * current + matmul_hi(couple, picked)

    row_top = lax.axis_size("row").bit_length() - 2
    for index_row in range(ROW_LEVELS):
        partner = from_partner(coeffs, "row", row_top - index_row)
        coeffs = mix_level(coeffs, partner, index_row)
    col_top = lax.axis_size("col").bit_length() - 2
    for index_col in range(COL_LEVELS):
        partner = from_partner(coeffs, "col", col_top - index_col)
        coeffs = mix_level(coeffs, partner, ROW_LEVELS + index_col)
    far_field = matmul_hi(expand, coeffs)
    weights = link_mask.astype(jnp.float32)
    near_scale = (3.0 * coords.shape[1]) ** (-0.5)
    near_field = matmul_hi(kernel_tile(coords, coords), residual_in)
    near_field = near_field + weights[0, 0] * matmul_hi(kernel_tile(coords, below_xyz), below_rhs)
    near_field = near_field + weights[0, 1] * matmul_hi(kernel_tile(coords, above_xyz), above_rhs)
    near_field = near_scale * near_field
    image = 2.0 * residual_in + near_field + far_field
    gram_mat = inner_cols(image, image)
    cross_mat = inner_cols(image, residual_in)
    points_total = coords.shape[1] * lax.axis_size("row") * lax.axis_size("col")
    self_squares = jnp.sum(residual_in * residual_in, axis=0)[None, :]
    gram_mat, cross_mat, self_total = global_sum((gram_mat, cross_mat, self_squares))
    alpha_mix = chol_solve(gram_mat, cross_mat)
    new_residual = residual_in - matmul_hi(image, alpha_mix)
    col_total = self_total[0] - jnp.sum(alpha_mix * cross_mat, axis=0)
    res_norms = jnp.sqrt(col_total / points_total)
    return (new_residual, res_norms)


def solution(mesh):
    return jax.shard_map(
        shards,
        mesh=mesh,
        in_specs=(
            P(None, ("row", "col")),
            P(("row", "col"), None),
            P(("row", "col"), None),
            P(("row", "col"), None),
            P(("row", "col"), None),
            P(("row", "col"), None),
            P(("row", "col"), None),
            P(("row", "col"), None, None),
        ),
        out_specs=(P(("row", "col"), None), P()),
        check_vma=False,
    )
```

profile of v0, /device:TPU:1, one launch (start us, length us, event | category | flops | bytes accessed | tf_op | source)
XLA Modules:
  0.0 549.9 jit_solution(8922406250387740012)
XLA Ops:
  7.2 4.6 collective-permute-start
  11.8 6.0 %collective-permute-start.2 = (f32[3,128]{1,0:T(4,128)}, f32[3,128]{1,0:T(4,128)}, u32[]{:S(2)}, u32[]{:S(2)}) collective-permute-start(f32[3,128]{1,0:T(4,128)} %param.10), channel_id=1, source_target_pairs={{1,0},{2,1},{3,2},{4,3},{5,4},{6,5},{7,6},{8,7},{9,8},{10,9},{11,1... | collective-permute-start | bytes 4616 | tf_op jit(solution)/shard_map/ppermute | solution.py:64
  17.9 1.9 collective-permute-start.1
  19.8 2.4 collective-permute-start.3
  23.8 16.8 %collective-permute-start.4 = (f32[256,512]{1,0:T(8,128)S(1)}, f32[256,512]{1,0:T(8,128)S(1)}, u32[]{:S(2)}, u32[]{:S(2)}) collective-permute-start(f32[256,512]{1,0:T(8,128)S(1)} %fusion.166), channel_id=1, source_target_pairs={{0,256},{256,0},{32,288},{288,32},{64,320},{320,64},{96,352},{352,... | collective-permute-start | bytes 1572872 | tf_op jit(solution)/shard_map/ppermute | solution.py:74
  45.5 8.0 %collective-permute-done.4 = f32[256,512]{1,0:T(8,128)S(1)} collective-permute-done((f32[256,512]{1,0:T(8,128)S(1)}, f32[256,512]{1,0:T(8,128)S(1)}, u32[]{:S(2)}, u32[]{:S(2)}) %collective-permute-start.4) | collective-permute-done | bytes 524320 | tf_op jit(solution)/shard_map/ppermute | solution.py:74
  56.2 36.6 %collective-permute-start.5 = (f32[256,512]{1,0:T(8,128)S(1)}, f32[256,512]{1,0:T(8,128)S(1)}, u32[]{:S(2)}, u32[]{:S(2)}) collective-permute-start(f32[256,512]{1,0:T(8,128)S(1)} %fusion), channel_id=1, source_target_pairs={{0,128},{128,0},{32,160},{160,32},{64,192},{192,64},{96,224},{224,... | collective-permute-start | bytes 1572872 | tf_op jit(solution)/shard_map/ppermute | solution.py:74
  92.8 42.3 %collective-permute-done.5 = f32[256,512]{1,0:T(8,128)S(1)} collective-permute-done((f32[256,512]{1,0:T(8,128)S(1)}, f32[256,512]{1,0:T(8,128)S(1)}, u32[]{:S(2)}, u32[]{:S(2)}) %collective-permute-start.5) | collective-permute-done | bytes 524320 | tf_op jit(solution)/shard_map/ppermute | solution.py:74
  141.2 13.1 %collective-permute-done.6 = f32[256,512]{1,0:T(8,128)S(1)} collective-permute-done((f32[256,512]{1,0:T(8,128)S(1)}, f32[256,512]{1,0:T(8,128)S(1)}, u32[]{:S(2)}, u32[]{:S(2)}) %collective-permute-start.6) | collective-permute-done | bytes 524320 | tf_op jit(solution)/shard_map/ppermute | solution.py:74
  161.7 9.3 %collective-permute-done.7 = f32[256,512]{1,0:T(8,128)S(1)} collective-permute-done((f32[256,512]{1,0:T(8,128)S(1)}, f32[256,512]{1,0:T(8,128)S(1)}, u32[]{:S(2)}, u32[]{:S(2)}) %collective-permute-start.7) | collective-permute-done | bytes 524320 | tf_op jit(solution)/shard_map/ppermute | solution.py:74
  173.8 2.1 collective-permute-start.8
  179.4 9.0 %collective-permute-done.8 = f32[256,512]{1,0:T(8,128)S(1)} collective-permute-done((f32[256,512]{1,0:T(8,128)S(1)}, f32[256,512]{1,0:T(8,128)S(1)}, u32[]{:S(2)}, u32[]{:S(2)}) %collective-permute-start.8) | collective-permute-done | bytes 524320 | tf_op jit(solution)/shard_map/ppermute | solution.py:74
  194.1 37.4 %all_to_all.11 = f32[32,1025,16]{1,2,0:T(8,128)S(1)} all-to-all(f32[32,1025,16]{1,2,0:T(8,128)S(1)} %maximum_bitcast_fusion), channel_id=1, replica_groups=mesh['row'=16,'col'=32] {'col'}, dimensions={0} | all-to-all | bytes 4198400 | tf_op jit(solution)/shard_map/all_to_all | solution.py:20
  232.9 66.4 %all_to_all.12 = f32[16,1,16400]{2,1,0:T(1,128)S(1)} all-to-all(f32[16,1,16400]{2,1,0:T(1,128)S(1)} %broadcast_in_dim.18), channel_id=1, replica_groups=mesh['row'=16,'col'=32] {'row'}, dimensions={0} | all-to-all | bytes 2099200 | tf_op jit(solution)/shard_map/all_to_all | solution.py:33
  301.2 48.2 %all-gather.2.cloned.1.call-done = f32[512,1025]{1,0:T(8,128)} async-done(((f32[16,1025]{1,0:T(8,128)}), f32[512,1025]{1,0:T(8,128)}) %all-gather.2.cloned.1.call-update) | async-done | bytes 2099216 | tf_op jit(solution)/shard_map/all_gather | solution.py:53
  349.5 2.4 slice_bitcast_fusion.1
  355.7 12.3 %cholesky.104 = f32[128,128]{1,0:T(8,128)} custom-call(f32[128,128]{1,0:T(8,128)S(1)} %cholesky.266), custom_call_target="Cholesky" | custom-call | tf_op jit(solution)/shard_map/jit(cholesky)/cholesky | solution.py:93
  370.4 11.3 %custom-call.32 = f32[1,128,128]{1,2,0:T(8,128)} custom-call(f32[1,128,128]{2,1,0:T(8,128)} %get-tuple-element.36), custom_call_target="InvertDiagBlocksLowerTriangular" | custom-call | tf_op jit(solution)/shard_map/jit(cholesky)/cholesky | solution.py:93
  385.5 13.2 %cholesky.217 = f32[128,128]{1,0:T(8,128)} custom-call(f32[128,128]{1,0:T(8,128)} %cholesky.270), custom_call_target="Cholesky" | custom-call | tf_op jit(solution)/shard_map/jit(cholesky)/cholesky | solution.py:93
  400.2 11.6 %custom-call.33 = f32[1,128,128]{1,2,0:T(8,128)} custom-call(f32[1,128,128]{2,1,0:T(8,128)} %get-tuple-element.33), custom_call_target="InvertDiagBlocksLowerTriangular" | custom-call | tf_op jit(solution)/shard_map/jit(cholesky)/cholesky | solution.py:93
  415.6 13.2 %cholesky.238 = f32[128,128]{1,0:T(8,128)} custom-call(f32[128,128]{1,0:T(8,128)} %cholesky.275), custom_call_target="Cholesky" | custom-call | tf_op jit(solution)/shard_map/jit(cholesky)/cholesky | solution.py:93
  430.9 11.3 %custom-call.34 = f32[1,128,128]{1,2,0:T(8,128)} custom-call(f32[1,128,128]{2,1,0:T(8,128)} %get-tuple-element.30), custom_call_target="InvertDiagBlocksLowerTriangular" | custom-call | tf_op jit(solution)/shard_map/jit(cholesky)/cholesky | solution.py:93
  445.1 13.3 %cholesky.255 = f32[128,128]{1,0:T(8,128)} custom-call(f32[128,128]{1,0:T(8,128)} %convolution_subtract_fusion.9), custom_call_target="Cholesky" | custom-call | tf_op jit(solution)/shard_map/jit(cholesky)/cholesky | solution.py:93
  464.3 14.2 %while.1 = (s32[]{:T(128)}, f32[512,512]{1,0:T(8,128)}, s32[4,2]{0,1:T(2,128)S(1)}, f32[4,128,128]{2,1,0:T(8,128)}, s32[]{:T(128)}) while((s32[]{:T(128)}, f32[512,512]{1,0:T(8,128)}, s32[4,2]{0,1:T(2,128)S(1)}, f32[4,128,128]{2,1,0:T(8,128)}, s32[]{:T(128)}) %tuple.50), condition=%wide.while_cond, body=%wide.while_body.sunk | while | flops 2 | bytes 132705 | solution.py:95
  464.9 2.9 bitcast_dynamic-update-slice_fusion.2
  468.5 2.9 bitcast_dynamic-update-slice_fusion.2
  472.1 2.9 bitcast_dynamic-update-slice_fusion.2
  475.6 2.8 bitcast_dynamic-update-slice_fusion.2
  478.5 40.7 %custom-call.35 = f32[4,128,128]{1,2,0:T(8,128)} custom-call(f32[4,128,128]{2,1,0:T(8,128)} %get-tuple-element.10), custom_call_target="InvertDiagBlocksLowerTriangular" | custom-call | tf_op jit(solution)/shard_map/triangular_solve | solution.py:95
  525.0 2.4 convolution_subtract_fusion.5
  532.3 2.3 convolution_subtract_fusion.4
  539.1 2.9 convolution_subtract_fusion.6
  (161 shorter events, 79.7 us)
Async XLA Ops:
  7.2 15.1 %copy-start = (f32[128,256]{1,0:T(8,128)S(1)}, f32[128,256]{1,0:T(8,128)}, u32[]{:S(2)}) copy-start(f32[128,256]{1,0:T(8,128)} %param.13) | copy-start | bytes 393220
  7.2 342.3 %all-gather.2.cloned.1.call-start = ((), (), s32[]{:S(2)}) async-start(), calls=%async_computation.2 | async-start | bytes 2433024 | tf_op jit(solution)/shard_map/all_gather | solution.py:53
  7.2 153.1 %collective-permute-start = (f32[3,128]{1,0:T(4,128)}, f32[3,128]{1,0:T(4,128)}, u32[]{:S(2)}, u32[]{:S(2)}) collective-permute-start(f32[3,128]{1,0:T(4,128)} %param.10), channel_id=1, source_target_pairs={{0,1},{1,2},{2,3},{3,4},{4,5},{5,6},{6,7},{7,8},{8,9},{9,10},{10,1... | collective-permute-start | bytes 4616 | tf_op jit(solution)/shard_map/ppermute | solution.py:64
  11.8 164.1 %collective-permute-start.2 = (f32[3,128]{1,0:T(4,128)}, f32[3,128]{1,0:T(4,128)}, u32[]{:S(2)}, u32[]{:S(2)}) collective-permute-start(f32[3,128]{1,0:T(4,128)} %param.10), channel_id=1, source_target_pairs={{1,0},{2,1},{3,2},{4,3},{5,4},{6,5},{7,6},{8,7},{9,8},{10,9},{11,1... | collective-permute-start | bytes 4616 | tf_op jit(solution)/shard_map/ppermute | solution.py:64
  17.9 158.8 %collective-permute-start.1 = (f32[128,512]{1,0:T(8,128)}, f32[128,512]{1,0:T(8,128)S(1)}, u32[]{:S(2)}, u32[]{:S(2)}) collective-permute-start(f32[128,512]{1,0:T(8,128)} %param.11), channel_id=1, source_target_pairs={{0,1},{1,2},{2,3},{3,4},{4,5},{5,6},{6,7},{7,8},{8,9},{9,10},{10,1... | collective-permute-start | bytes 786440 | tf_op jit(solution)/shard_map/ppermute | solution.py:64
  19.8 158.3 %collective-permute-start.3 = (f32[128,512]{1,0:T(8,128)}, f32[128,512]{1,0:T(8,128)S(1)}, u32[]{:S(2)}, u32[]{:S(2)}) collective-permute-start(f32[128,512]{1,0:T(8,128)} %param.11), channel_id=1, source_target_pairs={{1,0},{2,1},{3,2},{4,3},{5,4},{6,5},{7,6},{8,7},{9,8},{10,9},{11,1... | collective-permute-start | bytes 786440 | tf_op jit(solution)/shard_map/ppermute | solution.py:64
  23.8 29.7 %collective-permute-start.4 = (f32[256,512]{1,0:T(8,128)S(1)}, f32[256,512]{1,0:T(8,128)S(1)}, u32[]{:S(2)}, u32[]{:S(2)}) collective-permute-start(f32[256,512]{1,0:T(8,128)S(1)} %fusion.166), channel_id=1, source_target_pairs={{0,256},{256,0},{32,288},{288,32},{64,320},{320,64},{96,352},{352,... | collective-permute-start | bytes 1572872 | tf_op jit(solution)/shard_map/ppermute | solution.py:74
  56.2 79.0 %collective-permute-start.5 = (f32[256,512]{1,0:T(8,128)S(1)}, f32[256,512]{1,0:T(8,128)S(1)}, u32[]{:S(2)}, u32[]{:S(2)}) collective-permute-start(f32[256,512]{1,0:T(8,128)S(1)} %fusion), channel_id=1, source_target_pairs={{0,128},{128,0},{32,160},{160,32},{64,192},{192,64},{96,224},{224,... | collective-permute-start | bytes 1572872 | tf_op jit(solution)/shard_map/ppermute | solution.py:74
  136.1 4.3 copy-start.20
  136.2 4.3 copy-start.2
  137.9 16.4 %collective-permute-start.6 = (f32[256,512]{1,0:T(8,128)S(1)}, f32[256,512]{1,0:T(8,128)S(1)}, u32[]{:S(2)}, u32[]{:S(2)}) collective-permute-start(f32[256,512]{1,0:T(8,128)S(1)} %multiply_add_fusion.2), channel_id=1, source_target_pairs={{0,16},{16,0},{1,17},{17,1},{2,18},{18,2},{3,19},{19,3},{4,20},{20... | collective-permute-start | bytes 1572872 | tf_op jit(solution)/shard_map/ppermute | solution.py:74
  157.0 14.0 %collective-permute-start.7 = (f32[256,512]{1,0:T(8,128)S(1)}, f32[256,512]{1,0:T(8,128)S(1)}, u32[]{:S(2)}, u32[]{:S(2)}) collective-permute-start(f32[256,512]{1,0:T(8,128)S(1)} %multiply_add_fusion.1), channel_id=1, source_target_pairs={{0,8},{8,0},{1,9},{9,1},{2,10},{10,2},{3,11},{11,3},{4,12},{12,4},... | collective-permute-start | bytes 1572872 | tf_op jit(solution)/shard_map/ppermute | solution.py:74
  161.7 10.4 %copy-start.16 = (f32[1,256]{1,0:T(1,128)S(1)}, f32[1,256]{1,0:T(1,128)}, u32[]{:S(2)}) copy-start(f32[1,256]{1,0:T(1,128)} %get-tuple-element.39) | copy-start | bytes 3076
  172.1 4.6 copy-start.17
  172.1 4.6 copy-start.18
  172.1 4.6 copy-start.19
  173.8 14.6 %collective-permute-start.8 = (f32[256,512]{1,0:T(8,128)S(1)}, f32[256,512]{1,0:T(8,128)S(1)}, u32[]{:S(2)}, u32[]{:S(2)}) collective-permute-start(f32[256,512]{1,0:T(8,128)S(1)} %multiply_add_fusion), channel_id=1, source_target_pairs={{0,4},{4,0},{1,5},{5,1},{2,6},{6,2},{3,7},{7,3},{8,12},{12,8},{9,1... | collective-permute-start | bytes 1572872 | tf_op jit(solution)/shard_map/ppermute | solution.py:74
  179.4 10.1 %copy-start.21 = (pred[256]{0:T(512)(128)(4,1)S(1)}, pred[256]{0:T(512)(128)(4,1)}, u32[]{:S(2)}) copy-start(pred[256]{0:T(512)(128)(4,1)} %compare_and_fusion) | copy-start | bytes 772
  189.5 1.8 copy-start.14
  189.5 1.8 copy-start.15
  191.8 2.1 copy-start.5
  349.5 4.0 copy-start.1
  354.6 1.0 copy-start.7
  384.2 0.7 copy-start.12
  414.3 0.7 copy-start.13
  464.3 58.4 %copy-start.4 = (f32[512,512]{0,1:T(8,128)S(1)}, f32[512,512]{0,1:T(8,128)}, u32[]{:S(2)}) copy-start(f32[512,512]{0,1:T(8,128)} %get-tuple-element.22) | copy-start | bytes 3145732
  519.2 3.0 copy-start.9
  531.6 0.7 copy-start.8
  534.6 4.5 copy-start.3
  534.6 4.5 copy-start.6
  537.4 4.6 copy-start.10
  537.4 4.6 copy-start.11
Sparse Core Ops, SparseCore 0:
  301.4 48.0 all-gather.1
where the time goes:
time: 557 us; the launch traced here: 550 us
  other arithmetic  143 us (26%)
  waiting for transfers between devices  130 us (23%)
  blocking collectives  104 us (19%)
  starting transfers between devices  74.4 us (13%)
  matrix products  43 us (8%)
  local copies, waits for them, and re-layouts  38.3 us (7%)
  between operations  17.5 us (3%)
    another operation x14, other arithmetic, chol_solve(): factor = jnp.linalg.cholesky(gram_mat)  93.5 us
    ppermute x5, waiting for transfers between devices, from_partner(): return lax.ppermute(block, axis, route)  81.7 us
    all_to_all x1, blocking collectives, from_everyone(): lax.all_to_all(jnp.broadcast_to(shard[None], (length, *shard.shape)), axi...  66.4 us
    ppermute x5, starting transfers between devices, from_partner(): return lax.ppermute(block, axis, route)  59.3 us
    all_gather x1, waiting for transfers between devices, gather_turned(): lax.all_gather(both, axis, axis=0, tiled=True)  48.2 us
    another operation x3, other arithmetic, chol_solve(): lax.linalg.triangular_solve(factor, middle, left_side=True, lower=True, t...  41.9 us
    all_to_all x1, blocking collectives, sent_and_summed(): lax.all_to_all(in_blocks(shard, dim, length), axis, 0, 0, tiled=True)  37.4 us
    dot_general x10, matrix products, matmul_hi(): return jnp.dot(left, right, precision=lax.Precision.HIGHEST)  15.4 us
  transfers between devices with their start and end apart: 10, of which 6 were waited for; matrix products, arithmetic and copies ran while one was open for 5% of the time, Pallas kernels for 0%

commit v1 on v0

--- a/solution.py
+++ b/solution.py
@@ -50,7 +50,13 @@
 def gather_turned(arrays, axis, dims):
     turned = [jnp.moveaxis(a, dim, 0) for a, dim in zip(arrays, dims)]
     both = jnp.concatenate([t.reshape(len(t), -1) for t in turned], axis=1)
-    whole, at, finished = (lax.all_gather(both, axis, axis=0, tiled=True), 0, [])
+    whole, at, finished = (
+        jnp.concatenate(
+            lax.all_to_all(jnp.stack([both] * lax.axis_size(axis)), axis, 0, 0), axis=0
+        ),
+        0,
+        [],
+    )
     for t, dim in zip(turned, dims):
         piece = whole[:, at : at + t[0].size].reshape(-1, *t.shape[1:])
         finished.append(jnp.moveaxis(piece, 0, dim))

time: 557 us -> 533 us (0.957)
  waiting for transfers between devices: 130 us -> 112 us
  between operations: 17.5 us -> 4.08 us
    all_gather x1 -> x0, waiting for transfers between devices: 48.2 us -> none  [gather_turned(): lax.all_gather(both, axis, axis=0, tiled=True)]
    all_to_all x0 -> x1, waiting for transfers between devices: none -> 31 us  [gather_turned(): lax.all_to_all(jnp.stack([both] * lax.axis_size(axis)), axis, 0, 0)]
    another operation x12 -> x13, local copies, waits for them, and re-layouts: 14.2 us -> 15.6 us
where the time goes in v1:
time: 533 us; the launch traced here: 525 us
  other arithmetic  144 us (27%)
  waiting for transfers between devices  112 us (21%)
  blocking collectives  104 us (20%)
  starting transfers between devices  79.6 us (15%)
  matrix products  43.5 us (8%)
  local copies, waits for them, and re-layouts  39.1 us (7%)
    another operation x14, other arithmetic, chol_solve(): factor = jnp.linalg.cholesky(gram_mat)  93.6 us
    ppermute x5, waiting for transfers between devices, from_partner(): return lax.ppermute(block, axis, route)  80.9 us
    all_to_all x1, blocking collectives, from_everyone(): lax.all_to_all(jnp.broadcast_to(shard[None], (length, *shard.shape)), axi...  66.4 us
    ppermute x5, starting transfers between devices, from_partner(): return lax.ppermute(block, axis, route)  59.3 us
    another operation x3, other arithmetic, chol_solve(): lax.linalg.triangular_solve(factor, middle, left_side=True, lower=True, t...  41.9 us
    all_to_all x1, blocking collectives, sent_and_summed(): lax.all_to_all(in_blocks(shard, dim, length), axis, 0, 0, tiled=True)  37.4 us
    all_to_all x1, waiting for transfers between devices, gather_turned(): lax.all_to_all(jnp.stack([both] * lax.axis_size(axis)), axis, 0, 0)  31 us
    ppermute x4, starting transfers between devices, from_behind(): return lax.ppermute(block, axis, route)  15.1 us
  transfers between devices with their start and end apart: 10, of which 6 were waited for; matrix products, arithmetic and copies ran while one was open for 5% of the time, Pallas kernels for 0%

profile of v1, /device:TPU:1, one launch (start us, length us, event | category | flops | bytes accessed | tf_op | source)
XLA Modules:
  0.0 525.5 jit_solution(17205545126449687849)
XLA Ops:
  0.6 4.7 collective-permute-start
  5.4 6.1 %collective-permute-start.2 = (f32[3,128]{1,0:T(4,128)}, f32[3,128]{1,0:T(4,128)}, u32[]{:S(2)}, u32[]{:S(2)}) collective-permute-start(f32[3,128]{1,0:T(4,128)} %param.10), channel_id=1, source_target_pairs={{1,0},{2,1},{3,2},{4,3},{5,4},{6,5},{7,6},{8,7},{9,8},{10,9},{11,1... | collective-permute-start | bytes 4616 | tf_op jit(solution)/shard_map/ppermute | solution.py:70
  11.4 1.9 collective-permute-start.1
  13.4 2.4 collective-permute-start.3
  17.4 16.8 %collective-permute-start.4 = (f32[256,512]{1,0:T(8,128)S(1)}, f32[256,512]{1,0:T(8,128)S(1)}, u32[]{:S(2)}, u32[]{:S(2)}) collective-permute-start(f32[256,512]{1,0:T(8,128)S(1)} %fusion.166), channel_id=1, source_target_pairs={{0,256},{256,0},{32,288},{288,32},{64,320},{320,64},{96,352},{352,... | collective-permute-start | bytes 1572872 | tf_op jit(solution)/shard_map/ppermute | solution.py:80
  39.2 7.9 %collective-permute-done.4 = f32[256,512]{1,0:T(8,128)S(1)} collective-permute-done((f32[256,512]{1,0:T(8,128)S(1)}, f32[256,512]{1,0:T(8,128)S(1)}, u32[]{:S(2)}, u32[]{:S(2)}) %collective-permute-start.4) | collective-permute-done | bytes 524320 | tf_op jit(solution)/shard_map/ppermute | solution.py:80
  49.8 36.6 %collective-permute-start.5 = (f32[256,512]{1,0:T(8,128)S(1)}, f32[256,512]{1,0:T(8,128)S(1)}, u32[]{:S(2)}, u32[]{:S(2)}) collective-permute-start(f32[256,512]{1,0:T(8,128)S(1)} %fusion), channel_id=1, source_target_pairs={{0,128},{128,0},{32,160},{160,32},{64,192},{192,64},{96,224},{224,... | collective-permute-start | bytes 1572872 | tf_op jit(solution)/shard_map/ppermute | solution.py:80
  86.4 42.3 %collective-permute-done.5 = f32[256,512]{1,0:T(8,128)S(1)} collective-permute-done((f32[256,512]{1,0:T(8,128)S(1)}, f32[256,512]{1,0:T(8,128)S(1)}, u32[]{:S(2)}, u32[]{:S(2)}) %collective-permute-start.5) | collective-permute-done | bytes 524320 | tf_op jit(solution)/shard_map/ppermute | solution.py:80
  134.7 13.1 %collective-permute-done.6 = f32[256,512]{1,0:T(8,128)S(1)} collective-permute-done((f32[256,512]{1,0:T(8,128)S(1)}, f32[256,512]{1,0:T(8,128)S(1)}, u32[]{:S(2)}, u32[]{:S(2)}) %collective-permute-start.6) | collective-permute-done | bytes 524320 | tf_op jit(solution)/shard_map/ppermute | solution.py:80
  155.1 9.3 %collective-permute-done.7 = f32[256,512]{1,0:T(8,128)S(1)} collective-permute-done((f32[256,512]{1,0:T(8,128)S(1)}, f32[256,512]{1,0:T(8,128)S(1)}, u32[]{:S(2)}, u32[]{:S(2)}) %collective-permute-start.7) | collective-permute-done | bytes 524320 | tf_op jit(solution)/shard_map/ppermute | solution.py:80
  167.3 2.1 collective-permute-start.8
  170.2 2.0 fusion.4
  173.6 8.2 %collective-permute-done.8 = f32[256,512]{1,0:T(8,128)S(1)} collective-permute-done((f32[256,512]{1,0:T(8,128)S(1)}, f32[256,512]{1,0:T(8,128)S(1)}, u32[]{:S(2)}, u32[]{:S(2)}) %collective-permute-start.8) | collective-permute-done | bytes 524320 | tf_op jit(solution)/shard_map/ppermute | solution.py:80
  187.5 37.4 %all_to_all.16 = f32[32,1025,16]{1,2,0:T(8,128)S(1)} all-to-all(f32[32,1025,16]{1,2,0:T(8,128)S(1)} %maximum_bitcast_fusion), channel_id=1, replica_groups=mesh['row'=16,'col'=32] {'col'}, dimensions={0} | all-to-all | bytes 4198400 | tf_op jit(solution)/shard_map/all_to_all | solution.py:20
  226.3 66.4 %all_to_all.17 = f32[16,1,16400]{2,1,0:T(1,128)S(1)} all-to-all(f32[16,1,16400]{2,1,0:T(1,128)S(1)} %broadcast_in_dim.18), channel_id=1, replica_groups=mesh['row'=16,'col'=32] {'row'}, dimensions={0} | all-to-all | bytes 2099200 | tf_op jit(solution)/shard_map/all_to_all | solution.py:33
  295.5 5.1 all-to-all-start.2
  300.6 31.0 %all-to-all-done.2 = f32[32,16,1025]{2,1,0:T(8,128)S(1)} async-done(((f32[32,16,1025]{2,1,0:T(8,128)}), f32[32,16,1025]{2,1,0:T(8,128)S(1)}, u32[]{:S(2)}, u32[]{:S(2)}) %all-to-all-start.2) | async-done | bytes 2099232 | tf_op jit(solution)/shard_map/all_to_all | solution.py:55
  336.5 12.3 %cholesky.104 = f32[128,128]{1,0:T(8,128)} custom-call(f32[128,128]{1,0:T(8,128)S(1)} %cholesky.266), custom_call_target="Cholesky" | custom-call | tf_op jit(solution)/shard_map/jit(cholesky)/cholesky | solution.py:99
  351.3 11.3 %custom-call.32 = f32[1,128,128]{1,2,0:T(8,128)} custom-call(f32[1,128,128]{2,1,0:T(8,128)} %get-tuple-element.36), custom_call_target="InvertDiagBlocksLowerTriangular" | custom-call | tf_op jit(solution)/shard_map/jit(cholesky)/cholesky | solution.py:99
  366.4 13.2 %cholesky.217 = f32[128,128]{1,0:T(8,128)} custom-call(f32[128,128]{1,0:T(8,128)} %cholesky.270), custom_call_target="Cholesky" | custom-call | tf_op jit(solution)/shard_map/jit(cholesky)/cholesky | solution.py:99
  381.0 11.6 %custom-call.33 = f32[1,128,128]{1,2,0:T(8,128)} custom-call(f32[1,128,128]{2,1,0:T(8,128)} %get-tuple-element.33), custom_call_target="InvertDiagBlocksLowerTriangular" | custom-call | tf_op jit(solution)/shard_map/jit(cholesky)/cholesky | solution.py:99
  396.4 13.2 %cholesky.238 = f32[128,128]{1,0:T(8,128)} custom-call(f32[128,128]{1,0:T(8,128)} %cholesky.275), custom_call_target="Cholesky" | custom-call | tf_op jit(solution)/shard_map/jit(cholesky)/cholesky | solution.py:99
  411.8 11.3 %custom-call.34 = f32[1,128,128]{1,2,0:T(8,128)} custom-call(f32[1,128,128]{2,1,0:T(8,128)} %get-tuple-element.30), custom_call_target="InvertDiagBlocksLowerTriangular" | custom-call | tf_op jit(solution)/shard_map/jit(cholesky)/cholesky | solution.py:99
  426.0 13.2 %cholesky.255 = f32[128,128]{1,0:T(8,128)} custom-call(f32[128,128]{1,0:T(8,128)} %convolution_subtract_fusion.9), custom_call_target="Cholesky" | custom-call | tf_op jit(solution)/shard_map/jit(cholesky)/cholesky | solution.py:99
  445.2 14.0 %while.1 = (s32[]{:T(128)}, f32[512,512]{1,0:T(8,128)}, s32[4,2]{0,1:T(2,128)S(1)}, f32[4,128,128]{2,1,0:T(8,128)}, s32[]{:T(128)}) while((s32[]{:T(128)}, f32[512,512]{1,0:T(8,128)}, s32[4,2]{0,1:T(2,128)S(1)}, f32[4,128,128]{2,1,0:T(8,128)}, s32[]{:T(128)}) %tuple.50), condition=%wide.while_cond, body=%wide.while_body.sunk | while | flops 2 | bytes 132705 | solution.py:101
  445.9 2.9 bitcast_dynamic-update-slice_fusion.2
  449.4 2.9 bitcast_dynamic-update-slice_fusion.2
  452.9 2.9 bitcast_dynamic-update-slice_fusion.2
  456.5 2.8 bitcast_dynamic-update-slice_fusion.2
  459.2 40.7 %custom-call.35 = f32[4,128,128]{1,2,0:T(8,128)} custom-call(f32[4,128,128]{2,1,0:T(8,128)} %get-tuple-element.10), custom_call_target="InvertDiagBlocksLowerTriangular" | custom-call | tf_op jit(solution)/shard_map/triangular_solve | solution.py:101
  506.7 2.4 convolution_subtract_fusion.5
  513.9 2.3 convolution_subtract_fusion.4
  (155 shorter events, 85.2 us)
Async XLA Ops:
  0.6 15.2 %copy-start = (f32[128,256]{1,0:T(8,128)S(1)}, f32[128,256]{1,0:T(8,128)}, u32[]{:S(2)}) copy-start(f32[128,256]{1,0:T(8,128)} %param.13) | copy-start | bytes 393220
  0.6 153.1 %collective-permute-start = (f32[3,128]{1,0:T(4,128)}, f32[3,128]{1,0:T(4,128)}, u32[]{:S(2)}, u32[]{:S(2)}) collective-permute-start(f32[3,128]{1,0:T(4,128)} %param.10), channel_id=1, source_target_pairs={{0,1},{1,2},{2,3},{3,4},{4,5},{5,6},{6,7},{7,8},{8,9},{9,10},{10,1... | collective-permute-start | bytes 4616 | tf_op jit(solution)/shard_map/ppermute | solution.py:70
  5.4 164.0 %collective-permute-start.2 = (f32[3,128]{1,0:T(4,128)}, f32[3,128]{1,0:T(4,128)}, u32[]{:S(2)}, u32[]{:S(2)}) collective-permute-start(f32[3,128]{1,0:T(4,128)} %param.10), channel_id=1, source_target_pairs={{1,0},{2,1},{3,2},{4,3},{5,4},{6,5},{7,6},{8,7},{9,8},{10,9},{11,1... | collective-permute-start | bytes 4616 | tf_op jit(solution)/shard_map/ppermute | solution.py:70
  11.4 158.8 %collective-permute-start.1 = (f32[128,512]{1,0:T(8,128)}, f32[128,512]{1,0:T(8,128)S(1)}, u32[]{:S(2)}, u32[]{:S(2)}) collective-permute-start(f32[128,512]{1,0:T(8,128)} %param.11), channel_id=1, source_target_pairs={{0,1},{1,2},{2,3},{3,4},{4,5},{5,6},{6,7},{7,8},{8,9},{9,10},{10,1... | collective-permute-start | bytes 786440 | tf_op jit(solution)/shard_map/ppermute | solution.py:70
  13.4 158.8 %collective-permute-start.3 = (f32[128,512]{1,0:T(8,128)}, f32[128,512]{1,0:T(8,128)S(1)}, u32[]{:S(2)}, u32[]{:S(2)}) collective-permute-start(f32[128,512]{1,0:T(8,128)} %param.11), channel_id=1, source_target_pairs={{1,0},{2,1},{3,2},{4,3},{5,4},{6,5},{7,6},{8,7},{9,8},{10,9},{11,1... | collective-permute-start | bytes 786440 | tf_op jit(solution)/shard_map/ppermute | solution.py:70
  17.4 29.7 %collective-permute-start.4 = (f32[256,512]{1,0:T(8,128)S(1)}, f32[256,512]{1,0:T(8,128)S(1)}, u32[]{:S(2)}, u32[]{:S(2)}) collective-permute-start(f32[256,512]{1,0:T(8,128)S(1)} %fusion.166), channel_id=1, source_target_pairs={{0,256},{256,0},{32,288},{288,32},{64,320},{320,64},{96,352},{352,... | collective-permute-start | bytes 1572872 | tf_op jit(solution)/shard_map/ppermute | solution.py:80
  49.8 79.0 %collective-permute-start.5 = (f32[256,512]{1,0:T(8,128)S(1)}, f32[256,512]{1,0:T(8,128)S(1)}, u32[]{:S(2)}, u32[]{:S(2)}) collective-permute-start(f32[256,512]{1,0:T(8,128)S(1)} %fusion), channel_id=1, source_target_pairs={{0,128},{128,0},{32,160},{160,32},{64,192},{192,64},{96,224},{224,... | collective-permute-start | bytes 1572872 | tf_op jit(solution)/shard_map/ppermute | solution.py:80
  86.4 47.5 %copy-start.17 = (f32[3,128]{1,0:T(4,128)S(1)}, f32[3,128]{1,0:T(4,128)}, u32[]{:S(2)}) copy-start(f32[3,128]{1,0:T(4,128)} %param.10) | copy-start | bytes 4612
  86.4 47.5 %copy-start.1 = (f32[128,512]{1,0:T(8,128)S(1)}, f32[128,512]{1,0:T(8,128)}, u32[]{:S(2)}) copy-start(f32[128,512]{1,0:T(8,128)} %param.11) | copy-start | bytes 786436
  131.4 16.4 %collective-permute-start.6 = (f32[256,512]{1,0:T(8,128)S(1)}, f32[256,512]{1,0:T(8,128)S(1)}, u32[]{:S(2)}, u32[]{:S(2)}) collective-permute-start(f32[256,512]{1,0:T(8,128)S(1)} %multiply_add_fusion.2), channel_id=1, source_target_pairs={{0,16},{16,0},{1,17},{17,1},{2,18},{18,2},{3,19},{19,3},{4,20},{20... | collective-permute-start | bytes 1572872 | tf_op jit(solution)/shard_map/ppermute | solution.py:80
  150.5 14.0 %collective-permute-start.7 = (f32[256,512]{1,0:T(8,128)S(1)}, f32[256,512]{1,0:T(8,128)S(1)}, u32[]{:S(2)}, u32[]{:S(2)}) collective-permute-start(f32[256,512]{1,0:T(8,128)S(1)} %multiply_add_fusion.1), channel_id=1, source_target_pairs={{0,8},{8,0},{1,9},{9,1},{2,10},{10,2},{3,11},{11,3},{4,12},{12,4},... | collective-permute-start | bytes 1572872 | tf_op jit(solution)/shard_map/ppermute | solution.py:80
  155.1 10.4 %copy-start.16 = (f32[1,256]{1,0:T(1,128)S(1)}, f32[1,256]{1,0:T(1,128)}, u32[]{:S(2)}) copy-start(f32[1,256]{1,0:T(1,128)} %get-tuple-element.39) | copy-start | bytes 3076
  167.3 14.6 %collective-permute-start.8 = (f32[256,512]{1,0:T(8,128)S(1)}, f32[256,512]{1,0:T(8,128)S(1)}, u32[]{:S(2)}, u32[]{:S(2)}) collective-permute-start(f32[256,512]{1,0:T(8,128)S(1)} %multiply_add_fusion), channel_id=1, source_target_pairs={{0,4},{4,0},{1,5},{5,1},{2,6},{6,2},{3,7},{7,3},{8,12},{12,8},{9,1... | collective-permute-start | bytes 1572872 | tf_op jit(solution)/shard_map/ppermute | solution.py:80
  173.6 9.4 %copy-start.18 = (pred[256]{0:T(512)(128)(4,1)S(1)}, pred[256]{0:T(512)(128)(4,1)}, u32[]{:S(2)}) copy-start(pred[256]{0:T(512)(128)(4,1)} %compare_and_fusion) | copy-start | bytes 772
  173.6 11.1 %copy-start.14 = (f32[128,256]{1,0:T(8,128)S(1)}, f32[128,256]{1,0:T(8,128)}, u32[]{:S(2)}) copy-start(f32[128,256]{1,0:T(8,128)} %param.14) | copy-start | bytes 393220
  173.6 11.1 %copy-start.15 = (f32[1,256]{1,0:T(1,128)S(1)}, f32[1,256]{1,0:T(1,128)}, u32[]{:S(2)}) copy-start(f32[1,256]{1,0:T(1,128)} %get-tuple-element.37) | copy-start | bytes 3076
  185.2 2.1 copy-start.4
  295.5 36.1 %all-to-all-start.2 = ((f32[32,16,1025]{2,1,0:T(8,128)}), f32[32,16,1025]{2,1,0:T(8,128)S(1)}, u32[]{:S(2)}, u32[]{:S(2)}) async-start(f32[32,16,1025]{2,1,0:T(8,128)} %stack.2), calls=%async_computation.2 | async-start | bytes 4718592 | tf_op jit(solution)/shard_map/all_to_all | solution.py:55
  335.4 1.0 copy-start.6
  365.1 0.7 copy-start.12
  395.1 0.7 copy-start.13
  445.2 59.1 %copy-start.3 = (f32[512,512]{0,1:T(8,128)S(1)}, f32[512,512]{0,1:T(8,128)}, u32[]{:S(2)}) copy-start(f32[512,512]{0,1:T(8,128)} %get-tuple-element.22) | copy-start | bytes 3145732
  500.0 6.2 %copy-start.8 = (f32[4,128,128]{1,2,0:T(8,128)S(1)}, f32[4,128,128]{1,2,0:T(8,128)}, u32[]{:S(2)}) copy-start(f32[4,128,128]{1,2,0:T(8,128)} %custom-call.35) | copy-start | bytes 786436
  513.2 0.7 copy-start.7
  516.2 6.6 %copy-start.2 = (f32[128,512]{1,0:T(8,128)S(1)}, f32[128,512]{1,0:T(8,128)}, u32[]{:S(2)}) copy-start(f32[128,512]{1,0:T(8,128)} %param.11) | copy-start | bytes 786436
  516.2 6.6 %copy-start.5 = (f32[128,512]{1,0:T(8,128)S(1)}, f32[128,512]{1,0:T(8,128)}, u32[]{:S(2)}) copy-start(f32[128,512]{1,0:T(8,128)} %copy-done.4) | copy-start | bytes 786436
  518.9 3.9 copy-start.9
  519.7 3.1 copy-start.10
  519.7 3.1 copy-start.11
